TPU v7x, 32 devices: a whole 2x2x4 slice. The times are simulated.
32 devices in a mesh: section: 4 (over y, x), dp: 8 (over z, core).
Axes of the slice: x: 2, y: 2, z: 4, core: 2. Of those that a mesh axis runs over, the one named last changes fastest.
Arguments:
- tokens: bfloat16 [8192, 512], P('dp'), may hold values from -6 to 6
- cotangent: bfloat16 [8192, 512], P('dp'), may hold values from -6 to 6
- lengths: int32 [32, 16], P('dp'), may hold values from 0 to 256, as said below
- mat_a: float32 [4, 512, 2048], P('section', 'dp'), may hold values from -3 to 3
- mat_b: float32 [2, 2048, 512], P(None, 'dp', 'section'), may hold values from -0.125 to 0.125
- norms: float32 [4, 512, 2], P('section', 'dp'), may hold values from -1 to 3
- first_a: float32 [4, 512, 2048], P('section', 'dp'), may hold values from -0.005859375 to 0.005859375
- second_a: float32 [4, 512, 2048], P('section', 'dp'), may hold values from 1.5884231e-07 to 6.3536925e-07
- first_b: float32 [2, 2048, 512], P(None, 'dp', 'section'), may hold values from -0.005859375 to 0.005859375
- second_b: float32 [2, 2048, 512], P(None, 'dp', 'section'), may hold values from 1.5884231e-07 to 6.3536925e-07
- first_n: float32 [4, 512, 2], P('section', 'dp'), may hold values from -0.015625 to 0.015625
- second_n: float32 [4, 512, 2], P('section', 'dp'), may hold values from 1.4295807e-06 to 5.718323e-06
Outputs:
- grad_norm: float32 [], replicated
- output: bfloat16 [4, 2048, 512], P('section', 'dp')
- input_grad: float32 [4, 2048, 512], P('section', 'dp')
- clip_a: float32 [4, 512, 2048], P('section', 'dp')
- moment_a: float32 [4, 512, 2048], P('section', 'dp')
- square_a: float32 [4, 512, 2048], P('section', 'dp')
- master_a: float32 [4, 512, 2048], P('section', 'dp')
- copy_a: bfloat16 [4, 512, 2048], P('section', 'dp')
- clip_b: float32 [2, 2048, 512], P(None, 'dp', 'section')
- moment_b: float32 [2, 2048, 512], P(None, 'dp', 'section')
- square_b: float32 [2, 2048, 512], P(None, 'dp', 'section')
- master_b: float32 [2, 2048, 512], P(None, 'dp', 'section')
- copy_b: bfloat16 [2, 2048, 512], P(None, 'dp', 'section')
- clip_n: float32 [4, 512, 2], P('section', 'dp')
- moment_n: float32 [4, 512, 2], P('section', 'dp')
- square_n: float32 [4, 512, 2], P('section', 'dp')
- master_n: float32 [4, 512, 2], P('section', 'dp')
- copy_n: bfloat16 [4, 512, 2], P('section', 'dp')
Inputs may be any that keep to these rules, and one draw needn't show every extreme that they name: Each row packs sequences from the start of a micro-batch of 256 positions, the rest padding: either one sequence of 256 followed by zeros, or 16 lengths of 4 to 16. Some row is of the first kind in every draw.
All inputs are finite; a program needn't handle non-finite values.
Results may differ from a plain program's by a relative error of at most 0.022.
Values may be sent and summed in bfloat16 or wider, within the bound.
A program may use at most 256 MiB of HBM per device.

v0:
```python
import functools
import types

import jax
import jax.numpy as jnp
from jax import lax
from jax.experimental import pallas as pl
from jax.experimental.pallas import tpu as pltpu
from jax.sharding import PartitionSpec as P

HEADS = 8
STEP = 5


EPSILON = 1e-05
NEGATIVE = -1e30
CLIP_NORM = 1.0
BETA_ONE = 0.5
BETA_TWO = 0.5
ADAM_EPSILON = 1e-08
MATRIX_RATE = 0.05
NORM_RATE = 0.5
MATRIX_DECAY = 0.01


def norm_stats(value):
    centre = value - jnp.mean(value, -1, keepdims=True)
    inverse = lax.rsqrt(jnp.mean(centre * centre, -1, keepdims=True) + EPSILON)
    return (centre * inverse, inverse)


def norm_back(normal, inverse, upstream):
    return inverse * (
        upstream
        - jnp.mean(upstream, -1, keepdims=True)
        - normal * jnp.mean(upstream * normal, -1, keepdims=True)
    )


def adam_update(weight, moment_one, moment_two, gradient, step_rate, decay_rate):
    first_new = BETA_ONE * moment_one + (1.0 - BETA_ONE) * gradient
    second_new = BETA_TWO * moment_two + (1.0 - BETA_TWO) * gradient * gradient
    first_hat = first_new / (1.0 - BETA_ONE**STEP)
    second_hat = second_new / (1.0 - BETA_TWO**STEP)
    weight_new = weight - step_rate * (
        first_hat / (jnp.sqrt(second_hat) + ADAM_EPSILON) + decay_rate * weight
    )
    return (first_new, second_new, weight_new)


def segments_of(lengths_row, length):
    ends = jnp.cumsum(lengths_row, dtype=jnp.int32)
    places = jnp.arange(length, dtype=jnp.int32)
    segment = jnp.sum((ends[None, :] <= places[:, None]).astype(jnp.int32), axis=1, dtype=jnp.int32)
    live = (places < ends[-1]).astype(jnp.float32)
    return segment, live


def matmul(left, right, dims):
    return lax.dot_general(left, right, (dims, ((), ())), preferred_element_type=jnp.float32)


NN = ((1,), (0,))
NT = ((1,), (1,))
TN = ((0,), (0,))


def attention_forward(stream, weight, mask):
    length, width = stream.shape
    size = width // HEADS
    packed = matmul(stream, weight[:, : 3 * width], NN).astype(jnp.bfloat16)
    heads = packed.reshape(length, 3, HEADS, size)
    scores = jnp.einsum("qhd,khd->hqk", heads[:, 0], heads[:, 1], preferred_element_type=jnp.float32)
    scores = jnp.where(mask[None], scores * size**-0.5, NEGATIVE)
    weights = jnp.exp(scores - jnp.max(scores, -1, keepdims=True))
    probs = weights / jnp.sum(weights, -1, keepdims=True)
    mixed = jnp.einsum("hqk,khd->qhd", probs.astype(jnp.bfloat16), heads[:, 2], preferred_element_type=jnp.float32)
    mixed = mixed.reshape(length, width).astype(jnp.bfloat16)
    branch = matmul(mixed, weight[:, 3 * width :], NN)
    return branch, (heads, probs, mixed)


def attention_backward(stream, weight, kept, grad_low):
    heads, probs, mixed = kept
    length, width = stream.shape
    size = width // HEADS
    grad_out = matmul(mixed, grad_low, TN)
    grad_mixed = matmul(grad_low, weight[:, 3 * width :], NT).astype(jnp.bfloat16)
    grad_mixed = grad_mixed.reshape(length, HEADS, size)
    grad_probs = jnp.einsum("qhd,khd->hqk", grad_mixed, heads[:, 2], preferred_element_type=jnp.float32)
    centre = jnp.sum(probs * grad_probs, -1, keepdims=True)
    grad_scores = (probs * (grad_probs - centre)).astype(jnp.bfloat16)
    low = probs.astype(jnp.bfloat16)
    scale = size**-0.5
    grad_q = jnp.einsum("hqk,khd->qhd", grad_scores, heads[:, 1], preferred_element_type=jnp.float32) * scale
    grad_k = jnp.einsum("hqk,qhd->khd", grad_scores, heads[:, 0], preferred_element_type=jnp.float32) * scale
    grad_v = jnp.einsum("hqk,qhd->khd", low, grad_mixed, preferred_element_type=jnp.float32)
    packed = jnp.concatenate([grad_q, grad_k, grad_v], axis=1).reshape(length, 3 * width)
    packed = packed.astype(jnp.bfloat16)
    grad_in = matmul(stream, packed, TN)
    grad_inputs = matmul(packed, weight[:, : 3 * width], NT)
    return grad_inputs, jnp.concatenate([grad_in, grad_out], axis=1)


def feed_forward(stream, weight, down):
    pre = matmul(stream, weight, NN)
    active = jax.nn.gelu(pre, approximate=True).astype(jnp.bfloat16)
    return matmul(active, down, NN), (pre, active)


def feed_backward(stream, weight, down, kept, grad_low):
    pre, active = kept
    grad_down = matmul(active, grad_low, TN)
    grad_active = matmul(grad_low, down, NT)
    pull = jax.vjp(lambda value: jax.nn.gelu(value, approximate=True), pre)[1]
    grad_pre = pull(grad_active)[0].astype(jnp.bfloat16)
    grad_up = matmul(stream, grad_pre, TN)
    return matmul(grad_pre, weight, NT), grad_up, grad_down


def micro_step(rows, pull, segment, mats, downs, gains, biases):
    low = jnp.bfloat16
    mask = segment[:, None] == segment[None, :]
    stream, dual = rows, jnp.zeros_like(rows)
    saved = []
    for sub in range(4):
        if sub % 2 == 0:
            branch, kept = attention_forward(stream, mats[sub], mask)
        else:
            branch, kept = feed_forward(stream, mats[sub], downs[sub // 2])
        normal, inverse = norm_stats(stream.astype(jnp.float32) + branch)
        out = normal * gains[sub] + biases[sub]
        total = dual.astype(jnp.float32) + branch
        saved.append((stream, kept, normal, inverse))
        if sub < 3:
            stream, dual = out.astype(low), total.astype(low)
    dual_normal, dual_inverse = norm_stats(total)
    output = (out + dual_normal).astype(low)
    grad_out, grad_dual = pull, norm_back(dual_normal, dual_inverse, pull)
    grads_a, grads_b, grads_n = [None] * 4, [None] * 2, [None] * 4
    for sub in (3, 2, 1, 0):
        stream, kept, normal, inverse = saved[sub]
        grads_n[sub] = jnp.stack([jnp.sum(grad_out * normal, 0), jnp.sum(grad_out, 0)], axis=1)
        summed = norm_back(normal, inverse, grad_out * gains[sub])
        branch_low = (summed + grad_dual).astype(low)
        if sub % 2 == 0:
            inner, grads_a[sub] = attention_backward(stream, mats[sub], kept, branch_low)
        else:
            inner, grads_a[sub], grads_b[sub // 2] = feed_backward(
                stream, mats[sub], downs[sub // 2], kept, branch_low
            )
        grad_in = summed + inner
        if sub > 0:
            grad_out = grad_in.astype(low).astype(jnp.float32)
            grad_dual = grad_dual.astype(low).astype(jnp.float32)
    return output, grad_in, jnp.stack(grads_a), jnp.stack(grads_b), jnp.stack(grads_n)


def finish_step(grad_norm, output, input_grad, *groups):
    factor = CLIP_NORM / jnp.maximum(grad_norm, CLIP_NORM)
    results = [grad_norm, output[None], input_grad[None]]
    for weight, one, two, grad, rate, decay in groups:
        clip = grad * factor
        moment, square_new, master = adam_update(weight, one, two, clip, rate, decay)
        results += [clip, moment, square_new, master, master.astype(jnp.bfloat16)]
    return tuple(results)


def body(
    tokens, cotangent, lengths, mat_a, mat_b, norms, first_a, second_a, first_b, second_b, first_n, second_n
):
    low = jnp.bfloat16
    own = lax.axis_index("section")
    length = tokens.shape[0] // lengths.shape[0]
    rows = lax.dynamic_slice_in_dim(tokens, own * length, length, 0)
    segment, live = segments_of(lax.dynamic_index_in_dim(lengths, own, 0, keepdims=False), length)
    pull = lax.dynamic_slice_in_dim(cotangent, own * length, length, 0).astype(jnp.float32) * live[:, None]

    def gathered(value):
        return lax.all_gather(lax.all_gather(value, "dp", axis=1, tiled=True), "section", axis=0, tiled=True)

    mats = gathered(mat_a.astype(low))
    scales = gathered(norms.astype(low)).astype(jnp.float32)
    downs = lax.all_gather(mat_b.astype(low), "section", axis=2, tiled=True)
    downs = lax.all_gather(downs, "dp", axis=1, tiled=True)
    output, input_grad, part_a, part_b, part_n = micro_step(
        rows, pull, segment, mats, downs, scales[:, :, 0], scales[:, :, 1]
    )

    def scattered(value, section_dim):
        value = lax.psum_scatter(value, "section", scatter_dimension=section_dim, tiled=True)
        return lax.psum_scatter(value, "dp", scatter_dimension=1, tiled=True).astype(jnp.float32)

    grad_a = scattered(part_a.astype(low), 0)
    grad_b = scattered(part_b.astype(low), 2)
    grad_n = scattered(part_n, 0)
    square = jnp.sum(grad_a * grad_a) + jnp.sum(grad_b * grad_b) + jnp.sum(grad_n * grad_n)
    grad_norm = jnp.sqrt(lax.psum(square, ("section", "dp")))
    return finish_step(
        grad_norm, output, input_grad,
        (mat_a, first_a, second_a, grad_a, MATRIX_RATE, MATRIX_DECAY),
        (mat_b, first_b, second_b, grad_b, MATRIX_RATE, MATRIX_DECAY),
        (norms, first_n, second_n, grad_n, NORM_RATE, 0.0),
    )


LOW = jnp.bfloat16
WIDE = jnp.float32
MESH = pl.DeviceIdType.MESH
SECTIONS = 4
LANES = 128
BLOCK = 64
ROWS_FIRST = (5,)
KERNEL_VMEM = 64 * 1024 * 1024 - 256 * 1024


def gradient_items(rows_a, rows_b, cols_b, width, hidden):
    part = rows_a // SECTIONS
    return (
        ("B1", 3, cols_b // 2, rows_b),
        ("F3", 3, part, hidden // 2),
        ("O2", 2, part, width // 2),
        ("K2", 2, part, 3 * width // 2),
        ("B0", 1, cols_b // 2, rows_b),
        ("F1", 1, part, hidden // 2),
        ("O0", 0, part, width // 2),
        ("K0", 0, part, 3 * width // 2),
    )


def item_scratch(name, chips, rows, columns):
    piece = (rows, columns)
    return (
        ("own" + name, (chips, SECTIONS, 2) + piece, LOW),
        ("farx" + name, (chips,) + piece, LOW),
        ("fary" + name, (chips,) + piece, LOW),
        ("nearx" + name, (2, chips) + piece, LOW),
        ("neary" + name, (2, chips) + piece, LOW),
        ("line" + name, (chips, 2) + piece, LOW),
        ("done" + name, (2,) + piece if name[0] == "B" else (SECTIONS, 2) + piece, WIDE if name[0] == "B" else LOW),
    )


def kernel_scratch(chips, rows_a, rows_b, cols_b, length, width, hidden):
    devices = 2 * chips
    items = gradient_items(rows_a, rows_b, cols_b, width, hidden)
    count = len(items)
    received = sum((item_scratch(name, chips, rows, columns) for name, _, rows, columns in items), ())
    return received + (
        ("fac_s", (32,), None),
        ("fac_r", (32,), None),
        ("px_s", (count, 3), None),
        ("px_r", (count, 3), None),
        ("py_s", (count, 3), None),
        ("py_r", (count, 3), None),
        ("line_s", (count, chips), None),
        ("line_r", (count, chips), None),
        ("done_s", (count,), None),
        ("done_r", (count, SECTIONS), None),
        ("wa", (4, chips, 2, SECTIONS, rows_a // SECTIONS, hidden), LOW),
        ("wb", (2, chips, 2, SECTIONS, rows_b, cols_b), LOW),
        ("in_a", (1, rows_a, hidden), WIDE),
        ("in_b", (2, rows_b, cols_b), WIDE),
        ("in_n", (1, 2, rows_a), WIDE),
        ("out_a", (rows_a, hidden), WIDE),
        ("out_b", (2, rows_b, cols_b), WIDE),
        ("out_n", (2, rows_a), WIDE),
        ("out_square", (8, LANES), WIDE),
        ("out_output", (length, width), LOW),
        ("out_input", (length, width), WIDE),
        ("cut", (SECTIONS, rows_a // SECTIONS, hidden), LOW),
        ("tiles", (devices, SECTIONS, 8, LANES), WIDE),
        ("x", (4, length, width), LOW),
        ("xt", (4, chips, 2, rows_a, length), LOW),
        ("xtc", (4, chips, rows_a, 2 * length), LOW),
        ("y", (length, width), LOW),
        ("cot", (length, width), LOW),
        ("bias", (length, length), WIDE),
        ("live", (length, 1), WIDE),
        ("f", (length, width), WIDE),
        ("n", (4, length, width), WIDE),
        ("inv", (4, length, 1), WIDE),
        ("q", (2, length, width), LOW),
        ("k", (2, length, width), LOW),
        ("v", (2, length, width), LOW),
        ("kt", (2, width, length), LOW),
        ("vt", (2, width, length), LOW),
        ("ot", (2, chips, 2, rows_a, length), LOW),
        ("otc", (2, chips, rows_a, 2 * length), LOW),
        ("pt", (2, HEADS, length, length), LOW),
        ("g", (2, length, hidden), LOW),
        ("gc", (2, chips, 2 * length, rows_b), LOW),
        ("slope", (2, length, hidden), LOW),
        ("gx", (length, width), WIDE),
        ("gy", (length, width), WIDE),
        ("df", (2, 2 * length, width), LOW),
        ("dft", (2, width, 2 * length), LOW),
        ("dm", (length, width), LOW),
        ("dqt", (width, length), LOW),
        ("dh", (2, 2 * length, hidden), LOW),
        ("dp", (2, 2 * length, 3 * width), LOW),
        ("ng", (devices, 8, width), WIDE),
        ("ns", (SECTIONS, 8, width), WIDE),
        ("sq", (devices, 8, LANES), WIDE),
        ("sqs", (SECTIONS, 8, LANES), WIDE),
        ("sum", (8, LANES), WIDE),
        ("in_s", (5,), None),
        ("out_s", (6,), None),
        ("cut_s", (1,), None),
        ("cut_r", (SECTIONS,), None),
        ("gz_s", (6,), None),
        ("gz_r", (6, chips), None),
        ("gx_s", (6,), None),
        ("gx_r", (6,), None),
        ("gy_s", (6,), None),
        ("gy_r", (6,), None),
        ("rx_s", (6,), None),
        ("rx_r", (6,), None),
        ("ry_s", (6,), None),
        ("ry_r", (6,), None),
        ("gs_s", (6,), None),
        ("gs_r", (6,), None),
        ("small_s", (3, 2), None),
        ("small_r", (3, 2), None),
    )


INPUTS = ("tokens", "cotangent", "lengths", "mat_a", "mat_b", "norms")
OUTPUTS = ("grad_a", "grad_b", "grad_n", "square", "output", "input_grad")


def step_kernel(names, *refs):
    r = types.SimpleNamespace(**dict(zip(names, refs)))
    length, width = r.x.shape[1:]
    hidden = r.wa.shape[-1]
    rows_a, (rows_b, cols_b) = r.mat_a.shape[1], r.mat_b.shape[1:]
    devices = r.tiles.shape[0]
    chips = devices // 2
    half_b = cols_b // 2
    grad_items = gradient_items(rows_a, rows_b, cols_b, width, hidden)
    head = width // HEADS
    scale = head**-0.5

    s, d = lax.axis_index("section"), lax.axis_index("dp")
    z, c = lax.div(d, 2), lax.rem(d, 2)
    sx = s + 1 - 2 * lax.rem(s, 2)
    sy = lax.rem(s + 2, SECTIONS)
    sd = SECTIONS - 1 - s
    to_sibling = {"dp": d + 1 - 2 * c}
    to_up, to_down = {"dp": d + 2}, {"dp": d - 2}
    to_x, to_y = {"section": sx}, {"section": sy}
    below, above = z > 0, z < chips - 1
    group = [{"dp": lax.rem(d + step, devices)} for step in range(1, devices)]
    plane = [{"section": lax.rem(s + step, SECTIONS)} for step in range(1, SECTIONS)]
    finish = []

    def when(condition, work):
        if condition is None:
            work()
        else:
            pl.when(condition)(work)

    def push(source, target, send_sem, recv_sem, device):
        pltpu.make_async_remote_copy(
            src_ref=source,
            dst_ref=target,
            send_sem=send_sem,
            recv_sem=recv_sem,
            device_id=device,
            device_id_type=MESH,
        ).start()

    def arrived(target, sem):
        pltpu.make_async_remote_copy(
            src_ref=target, dst_ref=target, send_sem=sem, recv_sem=sem, device_id=to_x, device_id_type=MESH
        ).wait_recv()

    def sent(source, sem):
        pltpu.make_async_remote_copy(
            src_ref=source, dst_ref=source, send_sem=sem, recv_sem=sem, device_id=to_x, device_id_type=MESH
        ).wait_send()

    def at_end(condition, source, sem):
        finish.append((condition, source, sem))

    def aligned(start, size):
        return pl.ds(pl.multiple_of(start, size), size)

    own_x = pltpu.make_async_copy(r.tokens.at[aligned(s * length, length)], r.x.at[0], r.in_s.at[0])
    own_cot = pltpu.make_async_copy(r.cotangent.at[aligned(s * length, length)], r.cot, r.in_s.at[1])
    own_a = pltpu.make_async_copy(r.mat_a, r.in_a, r.in_s.at[2])
    own_b = pltpu.make_async_copy(r.mat_b, r.in_b, r.in_s.at[3])
    own_n = pltpu.make_async_copy(r.norms, r.in_n, r.in_s.at[4])
    own_a.start()
    own_n.start()
    own_b.start()
    own_x.start()
    own_cot.start()
    barrier = pltpu.get_barrier_semaphore()
    for peer in group + plane:
        pl.semaphore_signal(barrier, inc=1, device_id=peer, device_id_type=MESH)
    own_a.wait()
    r.cut[...] = r.in_a[0].astype(LOW).reshape(SECTIONS, rows_a // SECTIONS, hidden)
    r.wa[s, z, c, s] = r.cut[s]
    own_n.wait()
    norms = r.in_n[0].astype(LOW).astype(WIDE)
    nothing = jnp.zeros((2, rows_a), WIDE)
    even = jnp.concatenate([norms, nothing], axis=1)
    odd = jnp.concatenate([nothing, norms], axis=1)
    r.tiles[d, s, 0:2, :] = jnp.where(c == 0, even, odd)
    r.tiles[d, s, 2:8, :] = jnp.zeros((6, LANES), WIDE)
    own_b.wait()
    for layer in range(2):
        r.wb[layer, z, c, s] = r.in_b[layer].astype(LOW)
    pl.semaphore_wait(barrier, len(group) + len(plane))

    def put_out(slot, source, target):
        made = pltpu.make_async_copy(source, target, r.out_s.at[slot])
        made.start()
        return made

    def small_out(which, source):
        for peer in group:
            push(source, source, r.small_s.at[which, 0], r.small_r.at[which, 0], peer)

    def small_group(which, like):
        arrived(like, r.small_r.at[which, 0])
        sent(like, r.small_s.at[which, 0])

    def small_plane_out(which, source):
        for peer in plane:
            push(source, source, r.small_s.at[which, 1], r.small_r.at[which, 1], peer)

    def small_plane(which, like):
        arrived(like, r.small_r.at[which, 1])
        sent(like, r.small_s.at[which, 1])

    every = slice(None)

    def block(item, chip, section):
        if item < 4:
            return r.wa.at[item, chip, c, section]
        return r.wb.at[item - 4, chip, c, section]

    def half_block(item, section, half):
        if item < 4:
            return r.wa.at[item, :, c, section, :, pl.ds(half * hidden // 2, hidden // 2)]
        rows = pl.ds(half * rows_b // 2, rows_b // 2)
        return r.wb.at[item - 4, :, c, section, rows]

    def half_piece(item, section, half):
        rows = pl.ds(half * rows_b // 2, rows_b // 2)
        return r.wb.at[item - 4, z, c, section, rows]

    def core_blocks(item, core):
        return r.wa.at[item, :, core] if item < 4 else r.wb.at[item - 4, :, core]

    def cut_out():
        for section, device in ((sd, {"section": sd}), (sx, to_x), (sy, to_y)):
            push(r.cut.at[section], r.wa.at[s, z, c, section], r.cut_s.at[0], r.cut_r.at[s], device)
        at_end(None, r.cut.at[pl.ds(0, SECTIONS - 1)], r.cut_s.at[0])

    def cut_in():
        for section in (sx, sy, sd):
            arrived(r.wa.at[section, z, c, s], r.cut_r.at[section])

    def line_out(item):
        if item in ROWS_FIRST:
            rows_out(item)
            return
        own = block(item, z, s)
        for step in range(1, chips):
            push(own, own, r.gz_s.at[item], r.gz_r.at[item, z], {"dp": 2 * lax.rem(z + step, chips) + c})
        several = block(item, pl.ds(0, chips - 1), s)
        at_end(None, several, r.gz_s.at[item])

    def plane_out(item, chip):
        own = block(item, chip, s)
        push(own, own, r.gx_s.at[item], r.gx_r.at[item], to_x)
        push(own, own, r.gy_s.at[item], r.gy_r.at[item], to_y)

    def rows_out(item):
        arrived(half_piece(item, sd, 0), r.rx_r.at[item])
        arrived(half_piece(item, sd, 1), r.ry_r.at[item])
        rows = r.wb.at[item - 4, z, c]
        for step in range(1, chips):
            push(rows, rows, r.gz_s.at[item], r.gz_r.at[item, z], {"dp": 2 * lax.rem(z + step, chips) + c})
        push(rows, rows, r.gs_s.at[item], r.gs_r.at[item], to_sibling)
        at_end(None, r.wb.at[item - 4, pl.ds(0, chips - 1), c], r.gz_s.at[item])

    def rows_in(item):
        for step in range(1, chips):
            chip = lax.rem(z + step, chips)
            rows = r.wb.at[item - 4, chip, c]
            arrived(rows, r.gz_r.at[item, chip])
            push(rows, rows, r.gs_s.at[item], r.gs_r.at[item], to_sibling)
        at_end(None, core_blocks(item, c), r.gs_s.at[item])

    def line_in(item):
        if item in ROWS_FIRST:
            rows_in(item)
            return
        for step in range(1, chips):
            chip = lax.rem(z + step, chips)
            arrived(block(item, chip, s), r.gz_r.at[item, chip])
            plane_out(item, chip)
        core_out(item, s)
        at_end(None, block(item, every, s), r.gx_s.at[item])
        at_end(None, block(item, every, s), r.gy_s.at[item])

    def core_out(item, section):
        blocks = block(item, every, section)
        push(blocks, blocks, r.gs_s.at[item], r.gs_r.at[item], to_sibling)

    def plane_in(item):
        over = z if item in ROWS_FIRST else every
        piece = half_piece if item in ROWS_FIRST else half_block
        arrived(block(item, over, sx), r.gx_r.at[item])
        part = piece(item, sx, 1)
        push(part, part, r.ry_s.at[item], r.ry_r.at[item], to_y)
        arrived(block(item, over, sy), r.gy_r.at[item])
        part = piece(item, sy, 0)
        push(part, part, r.rx_s.at[item], r.rx_r.at[item], to_x)
        if item in ROWS_FIRST:
            at_end(None, block(item, z, sx), r.gx_s.at[item])
            at_end(None, block(item, z, sx), r.gy_s.at[item])
        else:
            core_out(item, sx)
            core_out(item, sy)
        at_end(None, part, r.ry_s.at[item])
        at_end(None, part, r.rx_s.at[item])

    def far_in(item):
        arrived(half_block(item, sd, 0), r.rx_r.at[item])
        arrived(half_block(item, sd, 1), r.ry_r.at[item])
        core_out(item, sd)
        at_end(None, core_blocks(item, c), r.gs_s.at[item])

    def core_in(item):
        arrived(core_blocks(item, 1 - c), r.gs_r.at[item])

    mine, other = pl.ds(0, length), pl.ds(length, length)

    def give(slot, source, target):
        push(source, target, r.fac_s.at[slot], r.fac_r.at[slot], to_sibling)
        at_end(None, target, r.fac_s.at[slot])

    def taken(slot, target):
        arrived(target, r.fac_r.at[slot])

    def give_rows(layer):
        r.xt[layer] = r.x[layer].T.reshape(chips, 2, rows_a, length)
        r.xtc[layer, :, :, 0:length] = r.xt[layer, :, c]
        give(layer, r.xt.at[layer, :, 1 - c], r.xtc.at[layer, :, :, other])

    def product(left, right, dims):
        return lax.dot_general(left, right, (dims, ((), ())), preferred_element_type=WIDE)

    def loop(count, work):
        def one(index, carry):
            work(index)
            return carry

        lax.fori_loop(0, count, one, 0)

    def gain_row(layer, kind):
        parts = [
            r.tiles[2 * chip, layer, kind : kind + 1, :] + r.tiles[2 * chip + 1, layer, kind : kind + 1, :]
            for chip in range(chips)
        ]
        return jnp.concatenate(parts, axis=1)

    def stats(value):
        centre = value - jnp.mean(value, -1, keepdims=True)
        inverse = lax.rsqrt(jnp.mean(centre * centre, -1, keepdims=True) + EPSILON)
        return centre * inverse, inverse

    lane = lax.broadcasted_iota(jnp.int32, (1, 2 * head), 1)
    first_half = (lane < head).astype(WIDE)
    half_masks = (first_half.astype(LOW), (1.0 - first_half).astype(LOW))

    def prepare_masks():
        ends, total = [], jnp.int32(0)
        for slot in range(r.lengths.shape[1]):
            total = total + r.lengths[s, slot]
            ends.append(total)
        down_places = lax.broadcasted_iota(jnp.int32, (length, 1), 0)
        across_places = lax.broadcasted_iota(jnp.int32, (1, length), 1)
        down_segment = jnp.zeros((length, 1), jnp.int32)
        across_segment = jnp.zeros((1, length), jnp.int32)
        for end in ends:
            down_segment = down_segment + (end <= down_places).astype(jnp.int32)
            across_segment = across_segment + (end <= across_places).astype(jnp.int32)
        r.bias[...] = jnp.where(down_segment == across_segment, 0.0, NEGATIVE)
        r.live[...] = (down_places < total).astype(WIDE)

    def matrix(layer, place):
        value = r.wa[layer, :, :, :, :, place]
        return value.reshape(width, value.shape[-1])

    def down(at, chip=slice(None)):
        blocks = [r.wb[at, chip, :, section] for section in range(SECTIONS)]
        return jnp.concatenate([block.reshape(-1, cols_b) for block in blocks], axis=1)

    def attention_in(layer):
        at = layer // 2
        rows = r.x[layer]
        r.q[at] = product(rows, matrix(layer, pl.ds(0, width)), NN).astype(LOW) * jnp.asarray(scale, LOW)
        keys = product(rows, matrix(layer, pl.ds(width, width)), NN).astype(LOW)
        r.k[at] = keys
        values = product(rows, matrix(layer, pl.ds(2 * width, width)), NN).astype(LOW)
        r.v[at] = values
        r.vt[at] = values.T

    def attention_heads(layer, begin, count):
        at = layer // 2

        def pair(index):
            lanes = aligned(index * 2 * head, 2 * head)
            for which in range(2):
                scores = product(r.k[at, :, lanes], r.q[at, :, lanes] * half_masks[which], NT) + r.bias[...]
                weights = jnp.exp(scores - jnp.max(scores, 0, keepdims=True))
                probs = (weights * (1.0 / jnp.sum(weights, 0, keepdims=True))).astype(LOW)
                r.pt[at, 2 * index + which] = probs
                place = aligned((2 * index + which) * head, head)
                r.ot[at, index, which] = product(r.vt[at, place, :], probs, NN).astype(LOW)

        for index in range(begin, begin + count):
            pair(index)

    def attention_out(layer):
        at = layer // 2
        r.otc[at, :, :, 0:length] = r.ot[at, :, c]
        give(4 + at, r.ot.at[at, :, 1 - c], r.otc.at[at, :, :, other])
        r.f[...] = product(r.ot[at].reshape(width, length).T, matrix(layer, pl.ds(3 * width, width)), NN)

    def expand(layer, index):
        at = layer // 2
        place = pl.ds(index * width, width)
        pre = product(r.x[layer], matrix(layer, place), NN)
        squared = pre * pre
        slope = 0.7978845608 * (1.0 + 3 * 0.044715 * squared)
        bent = jnp.tanh(0.7978845608 * pre * (1.0 + 0.044715 * squared))
        r.g[at, :, place] = (0.5 * pre * (1.0 + bent)).astype(LOW)
        r.slope[at, :, place] = (0.5 * (1.0 + bent) + 0.5 * pre * (1.0 - bent * bent) * slope).astype(LOW)
        block = aligned((2 * index + c) * rows_b, rows_b)
        r.gc[at, index, 0:length, :] = r.g[at, :, block]
        block = aligned((2 * index + 1 - c) * rows_b, rows_b)
        give(6 + chips * at + index, r.g.at[at, :, block], r.gc.at[at, index, other, :])

    def contract(layer):
        r.f[...] = product(r.g[layer // 2], down(layer // 2), NN)

    def by_rows(work):
        for index in range(length // BLOCK):
            work(pl.ds(index * BLOCK, BLOCK))

    def normalize(layer):
        gain, offset = gain_row(layer, 0), gain_row(layer, 1)

        def some(rows):
            branch = r.f[rows, :]
            normal, inverse = stats(r.x[layer, rows, :].astype(WIDE) + branch)
            r.n[layer, rows, :] = normal
            r.inv[layer, rows, :] = inverse
            out = normal * gain + offset
            dual = branch if layer == 0 else r.y[rows, :].astype(WIDE) + branch
            if layer < 3:
                r.x[layer + 1, rows, :] = out.astype(LOW)
                r.y[rows, :] = dual.astype(LOW)
            else:
                dual_normal, dual_inverse = stats(dual)
                r.out_output[rows, :] = (out + dual_normal).astype(LOW)
                pull = r.cot[rows, :].astype(WIDE) * r.live[rows, :]
                r.gx[rows, :] = pull
                r.gy[rows, :] = norm_back(dual_normal, dual_inverse, pull)

        by_rows(some)

    def back_normalize(layer):
        gain = gain_row(layer, 0)

        def some(index, sums):
            rows = pl.ds(index * BLOCK, BLOCK)
            upstream = r.gx[rows, :]
            normal = r.n[layer, rows, :]
            summed = norm_back(normal, r.inv[layer, rows, :], upstream * gain)
            dual = r.gy[rows, :]
            r.gx[rows, :] = summed
            r.df[layer // 2, rows, :] = (summed + dual).astype(LOW)
            if layer == 3:
                r.gy[rows, :] = dual.astype(LOW).astype(WIDE)
            return (
                sums[0] + jnp.sum(upstream * normal, 0, keepdims=True),
                sums[1] + jnp.sum(upstream, 0, keepdims=True),
            )

        zero = jnp.zeros((1, width), WIDE)
        gains, offsets = zero, zero
        for index in range(length // BLOCK):
            gains, offsets = some(index, (gains, offsets))
        r.ng[d, 2 * layer : 2 * layer + 1, :] = gains
        r.ng[d, 2 * layer + 1 : 2 * layer + 2, :] = offsets

    def pass_down(layer, inner):
        total = r.gx[...] + inner
        if layer > 0:
            r.gx[...] = total.astype(LOW).astype(WIDE)
        else:
            r.out_input[...] = total

    base = 6 + 2 * chips

    def back_hidden(layer):
        at = layer // 2
        r.dft[at, :, 0:length] = r.df[at, 0:length, :].T
        give(base + at, r.dft.at[at, :, mine], r.dft.at[at, :, other])
        for index in range(hidden // width):
            place = pl.ds(index * width, width)
            pulled = product(r.df[at, 0:length, :], down(at, pl.ds(index, 1)), NT)
            r.dh[at, 0:length, place] = (pulled * r.slope[at, :, place].astype(WIDE)).astype(LOW)
            give(base + 2 + chips * at + index, r.dh.at[at, mine, place], r.dh.at[at, other, place])

    def back_expand_end(layer):
        pass_down(layer, product(r.dh[layer // 2, 0:length, :], matrix(layer, pl.ds(0, hidden)), NT))

    def back_output(layer):
        at = layer // 2
        give(base + 2 + 2 * chips + at, r.df.at[at, mine], r.df.at[at, other])
        r.dm[...] = product(r.df[at, 0:length, :], matrix(layer, pl.ds(3 * width, width)), NT).astype(LOW)
        r.kt[at] = (r.k[at] * jnp.asarray(scale, LOW)).T

    def back_heads(layer, begin, count):
        at = layer // 2

        def pair(index):
            lanes = aligned(index * 2 * head, 2 * head)
            pulled = r.dm[:, lanes]
            keys, values = [], []
            for which in range(2):
                probs = r.pt[at, 2 * index + which]
                grad = product(r.v[at, :, lanes], pulled * half_masks[which], NT)
                full = probs.astype(WIDE)
                centre = jnp.sum(full * grad, 0, keepdims=True)
                scores = (full * (grad - centre)).astype(LOW)
                keys.append(product(scores, r.q[at, :, lanes], NN))
                values.append(product(probs, pulled, NN))
                place = aligned((2 * index + which) * head, head)
                r.dqt[place, :] = product(r.kt[at, place, :], scores, NN).astype(LOW)
            r.dp[at, 0:length, aligned(width + index * 2 * head, 2 * head)] = jnp.where(
                lane < head, keys[0], keys[1]
            ).astype(LOW)
            r.dp[at, 0:length, aligned(2 * width + index * 2 * head, 2 * head)] = jnp.where(
                lane < head, values[0], values[1]
            ).astype(LOW)

        def pairs(step):
            pair(begin + 2 * step)
            pair(begin + 2 * step + 1)

        loop(count // 2, pairs)

    def back_packed(layer):
        at = layer // 2
        slot = base + 4 + 2 * chips + 2 * at
        place = pl.ds(width, 2 * width)
        give(slot, r.dp.at[at, mine, place], r.dp.at[at, other, place])
        r.dp[at, 0:length, 0:width] = r.dqt[...].T
        place = pl.ds(0, width)
        give(slot + 1, r.dp.at[at, mine, place], r.dp.at[at, other, place])

    def back_packed_end(layer):
        pass_down(layer, product(r.dp[layer // 2, 0:length, :], matrix(layer, pl.ds(0, 3 * width)), NT))

    def keep(name, half, place, value):
        own = getattr(r, "own" + name)
        own[:, :, half, :, place] = value.astype(LOW).reshape(chips, SECTIONS, rows_a // SECTIONS, value.shape[1])

    def chip_rows(value):
        return value.reshape(chips * rows_a, 2 * length)

    def grad_down(at):
        own = getattr(r, "ownB%d" % at)
        taken(base + at, r.dft.at[at, :, other])
        for chip in range(chips):
            taken(6 + chips * at + chip, r.gc.at[at, chip, other, :])
            value = product(r.dft[at], r.gc[at, chip], NN)
            own[chip] = value.astype(LOW).reshape(SECTIONS, 2, half_b, rows_b)

    def grad_up(layer):
        at = layer // 2
        taken(layer, r.xtc.at[layer, :, :, other])
        for index in range(hidden // width):
            place = pl.ds(index * width, width)
            taken(base + 2 + chips * at + index, r.dh.at[at, other, place])
            value = product(chip_rows(r.xtc[layer]), r.dh[at, :, place], NN)
            keep("F%d" % layer, index // 2, pl.ds(index % 2 * width, width), value)

    def grad_output(layer):
        at = layer // 2
        taken(4 + at, r.otc.at[at, :, :, other])
        taken(base + 2 + 2 * chips + at, r.df.at[at, other])
        for half in range(2):
            place = pl.ds(half * width // 2, width // 2)
            value = product(chip_rows(r.otc[at]), r.df[at, :, place], NN)
            keep("O%d" % layer, half, pl.ds(0, width // 2), value)

    def grad_packed(layer):
        at = layer // 2
        slot = base + 4 + 2 * chips + 2 * at
        taken(layer, r.xtc.at[layer, :, :, other])
        taken(slot, r.dp.at[at, other, pl.ds(width, 2 * width)])
        taken(slot + 1, r.dp.at[at, other, pl.ds(0, width)])
        part = 3 * width // 2
        for half in range(2):
            value = product(chip_rows(r.xtc[layer]), r.dp[at, :, half * part : (half + 1) * part], NN)
            keep("K%d" % layer, half, pl.ds(0, part), value)

    def joined(target, others):
        return functools.reduce(
            lambda left, right: left + right, [ref[...].astype(WIDE) for ref in (target, *others)]
        )

    def add_into(target, others):
        if len(others) == 1:
            target[...] = target[...] + others[0][...]
        else:
            target[...] = joined(target, others).astype(LOW)

    places = {name: place for place, (name, _, _, _) in enumerate(grad_items)}

    def buffers(name):
        parts = ("own", "farx", "fary", "nearx", "neary", "line", "done")
        return types.SimpleNamespace(**{part: getattr(r, part + name) for part in parts})

    def to_plane(name):
        item, place = buffers(name), places[name]

        def over_x(section, half, target, slot):
            push(item.own.at[:, section, half], target, r.px_s.at[place, slot], r.px_r.at[place, slot], to_x)
            at_end(None, item.farx, r.px_s.at[place, slot])

        def over_y(section, half, target, slot):
            push(item.own.at[:, section, half], target, r.py_s.at[place, slot], r.py_r.at[place, slot], to_y)
            at_end(None, item.farx, r.py_s.at[place, slot])

        over_x(sd, 0, item.farx, 2)
        over_y(sd, 1, item.fary, 2)
        over_x(sx, 0, item.nearx.at[0], 0)
        over_y(sy, 1, item.neary.at[1], 1)

    def through_plane(name):
        item, place = buffers(name), places[name]
        own = item.own
        arrived(item.fary, r.py_r.at[place, 2])
        add_into(own.at[:, sx, 1], [item.fary])
        push(own.at[:, sx, 1], item.nearx.at[1], r.px_s.at[place, 1], r.px_r.at[place, 1], to_x)
        at_end(None, item.farx, r.px_s.at[place, 1])
        arrived(item.farx, r.px_r.at[place, 2])
        add_into(own.at[:, sy, 0], [item.farx])
        push(own.at[:, sy, 0], item.neary.at[0], r.py_s.at[place, 0], r.py_r.at[place, 0], to_y)
        at_end(None, item.farx, r.py_s.at[place, 0])

    def to_line(name):
        item, place = buffers(name), places[name]
        own = item.own.at[:, s]
        for half in range(2):
            arrived(item.nearx.at[half], r.px_r.at[place, half])
            arrived(item.neary.at[half], r.py_r.at[place, half])
            add_into(own.at[:, half], [item.nearx.at[half], item.neary.at[half]])
        for step in range(1, chips):
            chip = lax.rem(z + step, chips)
            push(
                own.at[chip],
                item.line.at[z],
                r.line_s.at[place, step],
                r.line_r.at[place, z],
                {"dp": 2 * chip + c},
            )
            at_end(None, item.line.at[0], r.line_s.at[place, step])

    def to_owner(name):
        item, place = buffers(name), places[name]
        others = [lax.rem(z + step, chips) for step in range(1, chips)]
        for chip in others:
            arrived(item.line.at[chip], r.line_r.at[place, chip])
        total = joined(item.own.at[z, s], [item.line.at[chip] for chip in others])
        square = total * total
        while square.ndim > 2:
            square = jnp.sum(square, 0)
        square = jnp.sum(jnp.sum(square, 0, keepdims=True), 1, keepdims=True)
        r.sum[...] = r.sum[...] + jnp.broadcast_to(square, (8, LANES))
        if name[0] == "B":
            item.done[...] = total
            return
        item.done[s] = total.astype(LOW)
        layer = grad_items[place][1]
        mine = item.done.at[s]
        away = s != layer
        when(
            away,
            lambda: push(mine, mine, r.done_s.at[place], r.done_r.at[place, s], {"section": jnp.int32(layer)}),
        )
        at_end(away, mine, r.done_s.at[place])

    def collect(name):
        item, place = buffers(name), places[name]
        layer = grad_items[place][1]

        def work():
            for section in range(SECTIONS):
                if section != layer:
                    arrived(item.done.at[section], r.done_r.at[place, section])
            columns = item.done.shape[-1]
            start = 3 * width if name[0] == "O" else 0
            for section in range(SECTIONS):
                for half in range(2):
                    rows = pl.ds(section * (rows_a // SECTIONS), rows_a // SECTIONS)
                    place_to = pl.ds(start + half * columns, columns)
                    r.out_a[rows, place_to] = item.done[section, half].astype(WIDE)

        when(s == layer, work)

    def all_sent(count=None):
        for condition, source, sem in finish[:count]:
            when(condition, functools.partial(sent, source, sem))
        del finish[:count]

    cut_out()
    small_out(0, r.tiles.at[d, s])
    plane_out(5, z)
    line_out(4)
    plane_out(4, z)
    cut_in()
    plane_out(1, z)
    line_out(0)
    plane_out(0, z)
    line_out(1)
    line_out(2)
    plane_out(3, z)
    line_out(3)
    line_in(4)
    small_group(0, r.tiles.at[pl.ds(0, devices - 1), 0])
    for peer in plane:
        push(r.tiles.at[:, s], r.tiles.at[:, s], r.small_s.at[0, 1], r.small_r.at[0, 1], peer)
    line_in(0)
    plane_in(5)
    line_in(1)
    plane_in(0)
    plane_out(2, z)
    plane_in(1)
    far_in(0)
    line_in(2)
    plane_in(4)
    line_out(5)
    own_x.wait()
    own_cot.wait()
    prepare_masks()
    core_in(0)
    attention_in(0)
    far_in(1)
    attention_heads(0, 0, 2)
    attention_heads(0, 2, 2)
    plane_in(2)
    attention_out(0)
    small_plane(0, r.tiles.at[:, pl.ds(0, SECTIONS - 1)])
    normalize(0)
    far_in(4)
    core_in(1)
    line_in(3)
    expand(1, 0)
    expand(1, 1)
    early = len(finish)
    far_in(2)
    expand(1, 2)
    expand(1, 3)
    core_in(4)
    contract(1)
    normalize(1)
    core_in(2)
    plane_in(3)
    attention_in(2)
    attention_heads(2, 0, 2)
    attention_heads(2, 2, 2)
    far_in(3)
    attention_out(2)
    line_in(5)
    normalize(2)
    core_in(3)
    expand(3, 0)
    expand(3, 1)
    expand(3, 2)
    expand(3, 3)
    all_sent(early)
    core_in(5)
    contract(3)
    normalize(3)
    leaving = [put_out(0, r.out_output, r.output)]

    r.sum[...] = jnp.zeros((8, LANES), WIDE)
    back_normalize(3)
    back_hidden(3)
    give_rows(3)
    back_expand_end(3)
    back_normalize(2)
    grad_up(3)
    to_plane("F3")
    back_output(2)
    grad_down(1)
    to_plane("B1")
    back_heads(2, 0, 2)
    back_heads(2, 2, 2)
    back_packed(2)
    through_plane("B1")
    give_rows(2)
    grad_output(2)
    back_packed_end(2)
    give_rows(1)
    to_plane("O2")
    grad_packed(2)
    to_plane("K2")
    back_normalize(1)
    back_hidden(1)
    through_plane("K2")
    grad_down(0)
    to_plane("B0")
    back_expand_end(1)
    back_normalize(0)
    small_out(1, r.ng.at[d])
    to_line("K2")
    to_line("B1")
    back_output(0)
    grad_up(1)
    through_plane("B0")
    to_plane("F1")
    back_heads(0, 0, 2)
    back_heads(0, 2, 2)
    back_packed(0)
    to_line("B0")
    through_plane("O2")
    through_plane("F1")
    grad_output(0)
    to_plane("O0")
    give_rows(0)
    grad_packed(0)
    to_plane("K0")
    to_line("O2")
    to_line("F1")
    through_plane("O0")
    to_owner("B1")
    back_packed_end(0)
    leaving.append(put_out(1, r.out_input, r.input_grad))
    to_owner("B0")
    all_sent()
    through_plane("K0")
    small_group(1, r.ng.at[pl.ds(0, devices - 1)])
    r.ns[s] = functools.reduce(lambda left, right: left + right, [r.ng[index] for index in range(devices)])
    small_plane_out(1, r.ns.at[s])
    through_plane("F3")
    to_line("O0")
    to_line("K0")
    to_owner("F1")
    to_line("F3")
    to_owner("O2")
    to_owner("K2")
    to_owner("F3")
    to_owner("O0")
    to_owner("K0")

    r.sq[d] = r.sum[...]
    small_out(2, r.sq.at[d])
    for name in ("F1", "O2", "K2", "F3"):
        collect(name)
    collect("O0")
    for layer in range(2):
        done = buffers("B%d" % layer).done
        r.out_b[layer] = done[...].reshape(cols_b, rows_b).T
    leaving.append(put_out(2, r.out_b, r.grad_b))
    small_plane(1, r.ns.at[pl.ds(0, SECTIONS - 1)])
    grads = functools.reduce(lambda left, right: left + right, [r.ns[index] for index in range(SECTIONS)])
    norm_square = jnp.sum(jnp.sum(grads * grads, 0, keepdims=True), 1, keepdims=True)
    chosen = jnp.zeros((2, width), WIDE)
    for layer in range(4):
        chosen = jnp.where(s == layer, grads[2 * layer : 2 * layer + 2, :], chosen)
    shard = jnp.zeros((2, rows_a), WIDE)
    for chip in range(chips):
        pair_of = chosen[:, chip * LANES : (chip + 1) * LANES]
        shard = jnp.where(z == chip, jnp.where(c == 0, pair_of[:, :rows_a], pair_of[:, rows_a:]), shard)
    r.out_n[...] = shard
    leaving.append(put_out(3, r.out_n, r.grad_n))
    collect("K0")
    leaving.append(put_out(4, r.out_a, r.grad_a))
    small_group(2, r.sq.at[pl.ds(0, devices - 1)])
    r.sqs[s] = functools.reduce(lambda left, right: left + right, [r.sq[index] for index in range(devices)])
    small_plane_out(2, r.sqs.at[s])
    all_sent()
    small_plane(2, r.sqs.at[pl.ds(0, SECTIONS - 1)])
    squares = functools.reduce(lambda left, right: left + right, [r.sqs[index] for index in range(SECTIONS)])
    r.out_square[...] = squares + norm_square
    leaving.append(put_out(5, r.out_square, r.square))
    for made in leaving:
        made.wait()


def step_call(tokens, cotangent, lengths, mat_a, mat_b, norms):
    rows_a, hidden = mat_a.shape[1:]
    rows_b, cols_b = mat_b.shape[1:]
    width = tokens.shape[1]
    length = tokens.shape[0] // lengths.shape[0]
    chips = width // rows_a // 2
    scratch = kernel_scratch(chips, rows_a, rows_b, cols_b, length, width, hidden)
    shapes = []
    for _, shape, kind in scratch:
        shapes.append(pltpu.SemaphoreType.DMA(shape) if kind is None else pltpu.VMEM(shape, kind))
    anywhere = pl.BlockSpec(memory_space=pl.ANY)
    return pl.pallas_call(
        functools.partial(step_kernel, INPUTS + OUTPUTS + tuple(name for name, _, _ in scratch)),
        out_shape=(
            jax.ShapeDtypeStruct((rows_a, hidden), WIDE),
            jax.ShapeDtypeStruct(mat_b.shape, WIDE),
            jax.ShapeDtypeStruct((2, rows_a), WIDE),
            jax.ShapeDtypeStruct((8, LANES), WIDE),
            jax.ShapeDtypeStruct((length, width), LOW),
            jax.ShapeDtypeStruct((length, width), WIDE),
        ),
        in_specs=[anywhere, anywhere, pl.BlockSpec(memory_space=pltpu.SMEM), anywhere, anywhere, anywhere],
        out_specs=[anywhere] * len(OUTPUTS),
        scratch_shapes=shapes,
        compiler_params=pltpu.CompilerParams(
            collective_id=0, has_side_effects=True, vmem_limit_bytes=KERNEL_VMEM
        ),
    )(tokens, cotangent, lengths, mat_a, mat_b, norms)


def update_kernel(*refs):
    inputs, outputs, held, made, sems = refs[:15], refs[15:33], refs[33:48], refs[48:63], refs[63]
    started = []

    def copy(source, target):
        one = pltpu.make_async_copy(source, target, sems.at[len(started)])
        one.start()
        started.append(one)
        return one

    half = inputs[4].shape[1] // 2
    parts = [(0, pl.ds(0, half)), (0, pl.ds(half, half)), (1, slice(None)), (2, slice(None))]
    rates = ((MATRIX_RATE, MATRIX_DECAY), (MATRIX_RATE, MATRIX_DECAY), (NORM_RATE, 0.0))
    norm_in = copy(inputs[0], held[0])
    coming = []
    for group, rows in parts:
        coming.append(
            [copy(inputs[at].at[:, rows], held[at].at[:, rows]) for at in range(3 + 4 * group, 7 + 4 * group)]
        )
    passing = [copy(inputs[at], held[at]) for at in (1, 2)]
    norm_in.wait()
    grad_norm = jnp.sqrt(held[0][0:1, 0:1])
    factor = CLIP_NORM / jnp.maximum(grad_norm, CLIP_NORM)
    outputs[0][...] = grad_norm
    leaving = []
    for (group, rows), waits in zip(parts, coming):
        for one in waits:
            one.wait()
        grad, weight, one, two = (held[at][:, rows] for at in range(3 + 4 * group, 7 + 4 * group))
        clip = grad * factor
        moment, square, master = adam_update(weight, one, two, clip, *rates[group])
        for kind, value in enumerate((clip, moment, square, master, master.astype(LOW))):
            buffer = made[5 * group + kind]
            buffer[:, rows] = value
            leaving.append(copy(buffer.at[:, rows], outputs[3 + 5 * group + kind].at[:, rows]))
        if passing:
            at = 3 - len(passing)
            passing.pop(0).wait()
            leaving.append(copy(held[at], outputs[at].at[0]))
    for one in leaving:
        one.wait()


def kernel_body(
    tokens, cotangent, lengths, mat_a, mat_b, norms, first_a, second_a, first_b, second_b, first_n, second_n
):
    norms, first_n, second_n = (jnp.swapaxes(value, 1, 2) for value in (norms, first_n, second_n))
    grad_a, grad_b, grad_n, square, output, input_grad = step_call(
        tokens, cotangent, lengths, mat_a, mat_b, norms
    )
    args = (square, output, input_grad, grad_a[None], mat_a, first_a, second_a, grad_b, mat_b, first_b, second_b)
    args += (grad_n[None], norms, first_n, second_n)
    anywhere, vmem = pl.BlockSpec(memory_space=pl.ANY), pl.BlockSpec(memory_space=pltpu.VMEM)
    shapes = [jax.ShapeDtypeStruct((1, 1), WIDE)]
    shapes += [jax.ShapeDtypeStruct((1,) + value.shape, value.dtype) for value in (output, input_grad)]
    for value in (mat_a, mat_b, norms):
        shapes += [jax.ShapeDtypeStruct(value.shape, kind) for kind in (WIDE, WIDE, WIDE, WIDE, LOW)]
    scratch = [pltpu.VMEM(value.shape, value.dtype) for value in (*args, *shapes[3:])]
    results = pl.pallas_call(
        update_kernel,
        out_shape=shapes,
        in_specs=[anywhere] * len(args),
        out_specs=[vmem] + [anywhere] * (len(shapes) - 1),
        scratch_shapes=scratch + [pltpu.SemaphoreType.DMA((48,))],
        compiler_params=pltpu.CompilerParams(vmem_limit_bytes=KERNEL_VMEM),
    )(*args)
    results = [results[0][0, 0], *results[1:]]
    results[-5:] = [jnp.swapaxes(value, 1, 2) for value in results[-5:]]
    return tuple(results)


def chosen_body(*args):
    rows_a = args[3].shape[1]
    groups = lax.axis_size("dp")
    by_kernel = rows_a % 32 == 0 and 2 * rows_a == LANES and groups * rows_a == args[0].shape[1]
    return (kernel_body if by_kernel else body)(*args)


def solution(mesh):
    placed = (
        P("dp", None),
        P("dp", None),
        P("dp", None),
        P("section", "dp", None),
        P(None, "dp", "section"),
        P("section", "dp", None),
        P("section", "dp", None),
        P("section", "dp", None),
        P(None, "dp", "section"),
        P(None, "dp", "section"),
        P("section", "dp", None),
        P("section", "dp", None),
    )
    return jax.shard_map(
        chosen_body,
        mesh=mesh,
        in_specs=placed,
        out_specs=(
            P(),
            P("section", "dp", None),
            P("section", "dp", None),
            P("section", "dp", None),
            P("section", "dp", None),
            P("section", "dp", None),
            P("section", "dp", None),
            P("section", "dp", None),
            P(None, "dp", "section"),
            P(None, "dp", "section"),
            P(None, "dp", "section"),
            P(None, "dp", "section"),
            P(None, "dp", "section"),
            P("section", "dp", None),
            P("section", "dp", None),
            P("section", "dp", None),
            P("section", "dp", None),
            P("section", "dp", None),
        ),
        check_vma=False,
    )
```

profile of v0, /device:TPU:0, one launch (start us, length us, event | category | flops | bytes accessed | tf_op | source)
XLA Modules:
  0.0 148.9 jit_solution(6981813313515983441)
XLA Ops:
  0.7 143.5 %shard_map.259 = (f32[64,2048]{1,0:T(8,128)}, f32[2,256,128]{2,1,0:T(8,128)}, f32[2,64]{1,0:T(2,128)}, f32[8,128]{1,0:T(8,128)}, bf16[256,512]{1,0:T(8,128)(2,1)}, /*index=5*/f32[256,512]{1,0:T(8,128)}) custom-call(bf16[1024,512]{1,0:T(8,128)(2,1)} %refs_0_.1, bf16[1024,512]{1,0:T(8,128)(2,1)} %refs_1_.1, s32[4,16]{1,0:T(4,128)} %refs_2_.1, ...), custom_call_target="tpu_custom_call" | custom-call | tf_op jit(solution)/shard_map/pallas_call | solution.py:1116
  144.2 4.6 %shard_map.260 = (f32[1,1]{1,0:T(1,128)}, bf16[1,256,512]{2,1,0:T(8,128)(2,1)}, f32[1,256,512]{2,1,0:T(8,128)}, f32[1,64,2048]{2,1,0:T(8,128)}, f32[1,64,2048]{2...) custom-call(f32[8,128]{1,0:T(8,128)} %get-tuple-element.42.refs_0_, ...), custom_call_target="tpu_custom_call" | custom-call | tf_op jit(solution)/shard_map/pallas_call | solution.py:1193
where the time goes:
time: 149 us
  Pallas kernels  148 us (99%)
    pallas_call x1, Pallas kernels, step_call(): pl.pallas_call(functools.partial(step_kernel, INPUTS + OUTPUTS + tuple((n...  144 us
    pallas_call x1, Pallas kernels, kernel_body(): pl.pallas_call(update_kernel, out_shape=shapes, in_specs=[anywhere] * len...  4.58 us

commit v1 on v0

--- a/solution.py
+++ b/solution.py
@@ -822,8 +822,8 @@
         )
 
     def add_into(target, others):
-        if len(others) == 1:
-            target[...] = target[...] + others[0][...]
+        if len(others) < 3:
+            target[...] = functools.reduce(lambda left, right: left + right, [ref[...] for ref in (target, *others)])
         else:
             target[...] = joined(target, others).astype(LOW)
 
@@ -956,6 +956,7 @@
     own_x.wait()
     own_cot.wait()
     prepare_masks()
+    give_rows(0)
     core_in(0)
     attention_in(0)
     far_in(1)
@@ -1041,7 +1042,6 @@
     through_plane("F1")
     grad_output(0)
     to_plane("O0")
-    give_rows(0)
     grad_packed(0)
     to_plane("K0")
     to_line("O2")
@@ -1051,13 +1051,14 @@
     back_packed_end(0)
     leaving.append(put_out(1, r.out_input, r.input_grad))
     to_owner("B0")
-    all_sent()
+    all_sent(len(finish) // 3)
     through_plane("K0")
     small_group(1, r.ng.at[pl.ds(0, devices - 1)])
     r.ns[s] = functools.reduce(lambda left, right: left + right, [r.ng[index] for index in range(devices)])
     small_plane_out(1, r.ns.at[s])
     through_plane("F3")
     to_line("O0")
+    all_sent(len(finish) // 3)
     to_line("K0")
     to_owner("F1")
     to_line("F3")
@@ -1065,6 +1066,7 @@
     to_owner("K2")
     to_owner("F3")
     to_owner("O0")
+    all_sent(len(finish) // 3)
     to_owner("K0")
 
     r.sq[d] = r.sum[...]

time: 149 us -> 149 us (level)
  no operation moved by 1% of the time
where the time goes in v1:
time: 149 us
  Pallas kernels  148 us (99%)
    pallas_call x1, Pallas kernels, step_call(): pl.pallas_call(functools.partial(step_kernel, INPUTS + OUTPUTS + tuple((n...  143 us
    pallas_call x1, Pallas kernels, kernel_body(): pl.pallas_call(update_kernel, out_shape=shapes, in_specs=[anywhere] * len...  4.58 us

profile of v1, /device:TPU:0, one launch (start us, length us, event | category | flops | bytes accessed | tf_op | source)
XLA Modules:
  0.0 148.6 jit_solution(16901526437259687752)
XLA Ops:
  0.7 143.2 %shard_map.259 = (f32[64,2048]{1,0:T(8,128)}, f32[2,256,128]{2,1,0:T(8,128)}, f32[2,64]{1,0:T(2,128)}, f32[8,128]{1,0:T(8,128)}, bf16[256,512]{1,0:T(8,128)(2,1)}, /*index=5*/f32[256,512]{1,0:T(8,128)}) custom-call(bf16[1024,512]{1,0:T(8,128)(2,1)} %refs_0_.1, bf16[1024,512]{1,0:T(8,128)(2,1)} %refs_1_.1, s32[4,16]{1,0:T(4,128)} %refs_2_.1, ...), custom_call_target="tpu_custom_call" | custom-call | tf_op jit(solution)/shard_map/pallas_call | solution.py:1118
  143.8 4.6 %shard_map.260 = (f32[1,1]{1,0:T(1,128)}, bf16[1,256,512]{2,1,0:T(8,128)(2,1)}, f32[1,256,512]{2,1,0:T(8,128)}, f32[1,64,2048]{2,1,0:T(8,128)}, f32[1,64,2048]{2...) custom-call(f32[8,128]{1,0:T(8,128)} %get-tuple-element.42.refs_0_, ...), custom_call_target="tpu_custom_call" | custom-call | tf_op jit(solution)/shard_map/pallas_call | solution.py:1195

commit v2 on v1

--- a/solution.py
+++ b/solution.py
@@ -556,13 +556,6 @@
     def product(left, right, dims):
         return lax.dot_general(left, right, (dims, ((), ())), preferred_element_type=WIDE)
 
-    def loop(count, work):
-        def one(index, carry):
-            work(index)
-            return carry
-
-        lax.fori_loop(0, count, one, 0)
-
     def gain_row(layer, kind):
         parts = [
             r.tiles[2 * chip, layer, kind : kind + 1, :] + r.tiles[2 * chip + 1, layer, kind : kind + 1, :]
@@ -616,13 +609,13 @@
         at = layer // 2
 
         def pair(index):
-            lanes = aligned(index * 2 * head, 2 * head)
+            lanes = pl.ds(index * 2 * head, 2 * head)
             for which in range(2):
                 scores = product(r.k[at, :, lanes], r.q[at, :, lanes] * half_masks[which], NT) + r.bias[...]
                 weights = jnp.exp(scores - jnp.max(scores, 0, keepdims=True))
                 probs = (weights * (1.0 / jnp.sum(weights, 0, keepdims=True))).astype(LOW)
                 r.pt[at, 2 * index + which] = probs
-                place = aligned((2 * index + which) * head, head)
+                place = pl.ds((2 * index + which) * head, head)
                 r.ot[at, index, which] = product(r.vt[at, place, :], probs, NN).astype(LOW)
 
         for index in range(begin, begin + count):
@@ -734,7 +727,7 @@
         at = layer // 2
 
         def pair(index):
-            lanes = aligned(index * 2 * head, 2 * head)
+            lanes = pl.ds(index * 2 * head, 2 * head)
             pulled = r.dm[:, lanes]
             keys, values = [], []
             for which in range(2):
@@ -745,20 +738,17 @@
                 scores = (full * (grad - centre)).astype(LOW)
                 keys.append(product(scores, r.q[at, :, lanes], NN))
                 values.append(product(probs, pulled, NN))
-                place = aligned((2 * index + which) * head, head)
+                place = pl.ds((2 * index + which) * head, head)
                 r.dqt[place, :] = product(r.kt[at, place, :], scores, NN).astype(LOW)
-            r.dp[at, 0:length, aligned(width + index * 2 * head, 2 * head)] = jnp.where(
+            r.dp[at, 0:length, pl.ds(width + index * 2 * head, 2 * head)] = jnp.where(
                 lane < head, keys[0], keys[1]
             ).astype(LOW)
-            r.dp[at, 0:length, aligned(2 * width + index * 2 * head, 2 * head)] = jnp.where(
+            r.dp[at, 0:length, pl.ds(2 * width + index * 2 * head, 2 * head)] = jnp.where(
                 lane < head, values[0], values[1]
             ).astype(LOW)
 
-        def pairs(step):
-            pair(begin + 2 * step)
-            pair(begin + 2 * step + 1)
-
-        loop(count // 2, pairs)
+        for index in range(begin, begin + count):
+            pair(index)
 
     def back_packed(layer):
         at = layer // 2
@@ -927,10 +917,10 @@
         del finish[:count]
 
     cut_out()
-    small_out(0, r.tiles.at[d, s])
     plane_out(5, z)
     line_out(4)
     plane_out(4, z)
+    small_out(0, r.tiles.at[d, s])
     cut_in()
     plane_out(1, z)
     line_out(0)

time: 149 us -> 149 us (level)
  no operation moved by 1% of the time
where the time goes in v2:
time: 149 us
  Pallas kernels  148 us (99%)
    pallas_call x1, Pallas kernels, step_call(): pl.pallas_call(functools.partial(step_kernel, INPUTS + OUTPUTS + tuple((n...  143 us
    pallas_call x1, Pallas kernels, kernel_body(): pl.pallas_call(update_kernel, out_shape=shapes, in_specs=[anywhere] * len...  4.58 us

profile of v2, /device:TPU:0, one launch (start us, length us, event | category | flops | bytes accessed | tf_op | source)
XLA Modules:
  0.0 148.6 jit_solution(3293610224157500699)
XLA Ops:
  0.7 143.2 %shard_map.259 = (f32[64,2048]{1,0:T(8,128)}, f32[2,256,128]{2,1,0:T(8,128)}, f32[2,64]{1,0:T(2,128)}, f32[8,128]{1,0:T(8,128)}, bf16[256,512]{1,0:T(8,128)(2,1)}, /*index=5*/f32[256,512]{1,0:T(8,128)}) custom-call(bf16[1024,512]{1,0:T(8,128)(2,1)} %refs_0_.1, bf16[1024,512]{1,0:T(8,128)(2,1)} %refs_1_.1, s32[4,16]{1,0:T(4,128)} %refs_2_.1, ...), custom_call_target="tpu_custom_call" | custom-call | tf_op jit(solution)/shard_map/pallas_call | solution.py:1108
  143.8 4.6 %shard_map.260 = (f32[1,1]{1,0:T(1,128)}, bf16[1,256,512]{2,1,0:T(8,128)(2,1)}, f32[1,256,512]{2,1,0:T(8,128)}, f32[1,64,2048]{2,1,0:T(8,128)}, f32[1,64,2048]{2...) custom-call(f32[8,128]{1,0:T(8,128)} %get-tuple-element.42.refs_0_, ...), custom_call_target="tpu_custom_call" | custom-call | tf_op jit(solution)/shard_map/pallas_call | solution.py:1185

commit v3 on v2

--- a/solution.py
+++ b/solution.py
@@ -595,6 +595,9 @@
         blocks = [r.wb[at, chip, :, section] for section in range(SECTIONS)]
         return jnp.concatenate([block.reshape(-1, cols_b) for block in blocks], axis=1)
 
+    def turn_keys(at):
+        r.kt[at] = (r.k[at] * jnp.asarray(scale, LOW)).T
+
     def attention_in(layer):
         at = layer // 2
         rows = r.x[layer]
@@ -721,7 +724,6 @@
         at = layer // 2
         give(base + 2 + 2 * chips + at, r.df.at[at, mine], r.df.at[at, other])
         r.dm[...] = product(r.df[at, 0:length, :], matrix(layer, pl.ds(3 * width, width)), NT).astype(LOW)
-        r.kt[at] = (r.k[at] * jnp.asarray(scale, LOW)).T
 
     def back_heads(layer, begin, count):
         at = layer // 2
@@ -982,6 +984,10 @@
     expand(3, 1)
     expand(3, 2)
     expand(3, 3)
+    for layer in (3, 2, 1):
+        give_rows(layer)
+    for at in (1, 0):
+        turn_keys(at)
     all_sent(early)
     core_in(5)
     contract(3)
@@ -991,7 +997,6 @@
     r.sum[...] = jnp.zeros((8, LANES), WIDE)
     back_normalize(3)
     back_hidden(3)
-    give_rows(3)
     back_expand_end(3)
     back_normalize(2)
     grad_up(3)
@@ -1003,10 +1008,8 @@
     back_heads(2, 2, 2)
     back_packed(2)
     through_plane("B1")
-    give_rows(2)
     grad_output(2)
     back_packed_end(2)
-    give_rows(1)
     to_plane("O2")
     grad_packed(2)
     to_plane("K2")

time: 149 us -> 149 us (level)
  no operation moved by 1% of the time
where the time goes in v3:
time: 149 us
  Pallas kernels  148 us (99%)
    pallas_call x1, Pallas kernels, step_call(): pl.pallas_call(functools.partial(step_kernel, INPUTS + OUTPUTS + tuple((n...  144 us
    pallas_call x1, Pallas kernels, kernel_body(): pl.pallas_call(update_kernel, out_shape=shapes, in_specs=[anywhere] * len...  4.58 us

profile of v3, /device:TPU:0, one launch (start us, length us, event | category | flops | bytes accessed | tf_op | source)
XLA Modules:
  0.0 149.3 jit_solution(18267601868155358896)
XLA Ops:
  0.7 143.9 %shard_map.259 = (f32[64,2048]{1,0:T(8,128)}, f32[2,256,128]{2,1,0:T(8,128)}, f32[2,64]{1,0:T(2,128)}, f32[8,128]{1,0:T(8,128)}, bf16[256,512]{1,0:T(8,128)(2,1)}, /*index=5*/f32[256,512]{1,0:T(8,128)}) custom-call(bf16[1024,512]{1,0:T(8,128)(2,1)} %refs_0_.1, bf16[1024,512]{1,0:T(8,128)(2,1)} %refs_1_.1, s32[4,16]{1,0:T(4,128)} %refs_2_.1, ...), custom_call_target="tpu_custom_call" | custom-call | tf_op jit(solution)/shard_map/pallas_call | solution.py:1111
  144.5 4.6 %shard_map.260 = (f32[1,1]{1,0:T(1,128)}, bf16[1,256,512]{2,1,0:T(8,128)(2,1)}, f32[1,256,512]{2,1,0:T(8,128)}, f32[1,64,2048]{2,1,0:T(8,128)}, f32[1,64,2048]{2...) custom-call(f32[8,128]{1,0:T(8,128)} %get-tuple-element.42.refs_0_, ...), custom_call_target="tpu_custom_call" | custom-call | tf_op jit(solution)/shard_map/pallas_call | solution.py:1188
